TPU v7x, 32 devices: a whole 2x2x4 slice. The times are simulated.
32 devices in a mesh: pencil: 8 (over z, y), lev: 4 (over x, core).
Axes of the slice: x: 2, y: 2, z: 4, core: 2. Of those that a mesh axis runs over, the one named last changes fastest.
Arguments:
- background_std: float32 [4, 4096, 2048], P('lev', 'pencil'), may hold values from 0.4 to 6.1
- x_kernel: float32 [4, 31], P('lev'), may hold values from -0.06 to 0.12
- y_kernel: float32 [4, 31], P('lev'), may hold values from -0.06 to 0.12
- obs_owner: int32 [8192, 1], P(('pencil', 'lev')), may hold values from 0 to 7; in each aligned block of 256 rows (0 to 255, 256 to 511, ...) at most 64 rows name the same one
- obs_cells: int32 [8192, 16], P(('pencil', 'lev')), may hold values from 0 to 1048575, as said below
- obs_weights: float32 [8192, 16], P(('pencil', 'lev')), may hold values from -0.05 to 0.2
- innovation: float32 [8192], P(('pencil', 'lev')), may hold values from -6 to 6
- obs_precision: float32 [8192], P(('pencil', 'lev')), may hold values from 0.25 to 4
- obs_counts: int32 [32], P(('pencil', 'lev')), may hold values from 129 to 256, as said below
Outputs:
- control: float32 [4, 2048, 4096], P('lev', 'pencil')
- increment: float32 [4, 4096, 2048], P('lev', 'pencil')
Inputs may be any that keep to these rules, and one draw needn't show every extreme that they name: `obs_owner`: no device holds more than 64 observations of one owner, and some device reaches 64. `obs_cells`: indices into the owner's tile of 1 slabs by 512 columns by 2048 rows, flattened in that order. `obs_counts`: some device has all 256 slots live.
All inputs are finite; a program needn't handle non-finite values.
Results may differ from a plain program's by a relative error of at most 0.0001.
Values sent between devices are 32-bit elements; how exact they have to be, the bound alone decides.
No kernel may reach another device: no remote copies, remote signals or barrier semaphores. Data moves between devices by JAX's collectives and lax.ppermute only.
A program may use at most 64 MiB of HBM per device.

v0:
```python
import functools

import jax
import jax.numpy as jnp
import numpy as np
from jax import lax
from jax.experimental import pallas as pl
from jax.experimental.pallas import tpu as pltpu
from jax.sharding import PartitionSpec as P


BF = jnp.bfloat16
F32 = jnp.float32
I32 = jnp.int32
LANES = 128
WIDE = 256
HALO = 32
PAD = 16
PACK = 40
GROUP = 8
PAIR = 2
BATCH = 4
BLOCK = 32
CODES = 40
STACK = 64
LISTED = 512
VMEM_LIMIT = 58 * 1024 * 1024


def vmem():
    return pl.BlockSpec(memory_space=pltpu.VMEM)


def smem():
    return pl.BlockSpec(memory_space=pltpu.SMEM)


def hbm():
    return pl.BlockSpec(memory_space=pl.ANY)


def cost(nanoseconds):
    return pl.CostEstimate(flops=0, bytes_accessed=3690 * nanoseconds, transcendentals=0)


def params():
    return pltpu.CompilerParams(vmem_limit_bytes=VMEM_LIMIT)


def split2(x):
    high = x.astype(BF)
    return high, (x - high.astype(F32)).astype(BF)


def split3(x):
    high = x.astype(BF)
    rest = x - high.astype(F32)
    mid = rest.astype(BF)
    return high, mid, (rest - mid.astype(F32)).astype(BF)


def mm(a, b):
    return jnp.dot(a, b, preferred_element_type=F32)


def mm_parts(a_parts, b_parts):
    (ah, al), (bh, bl) = a_parts, b_parts
    return mm(jnp.concatenate([ah, al, ah], axis=1), jnp.concatenate([bh, bh, bl], axis=0))


def iota(shape, dim):
    return lax.broadcasted_iota(I32, shape, dim)


def pack_kernel(
    counts, owner, cells, weights, depart, prec, out, marks, *, parts, columns, height, margin
):
    stencil, hold = cells.shape
    shift = height.bit_length() - 1
    block = height // parts
    reach = 2 * margin
    row_id = iota((hold, hold), 0)
    col_id = iota((hold, hold), 1)
    eye = row_id == col_id
    col_f = col_id.astype(F32)
    live = iota((1, hold), 1) < counts[0]
    cell = cells[...]
    column = lax.shift_right_logical(cell, jnp.full(cell.shape, shift, I32))
    row = cell & (height - 1)

    def any_of(mask):
        return jnp.max(jnp.where(mask, 1.0, 0.0), axis=0, keepdims=True)

    def turn(line):
        return jnp.sum(jnp.where(eye, line, 0.0), axis=1, keepdims=True)

    left = any_of(column < reach)
    right = any_of(column >= columns - reach)
    side = left + 3.0 * right - 2.0 * left * right
    base = jnp.where(live, owner[...].astype(F32) * 4.0, 4.0 * parts)
    key = jnp.where(live, base + side, base)
    key_col = turn(key)
    before = (key_col < key) | ((key_col == key) & (row_id < col_id))
    rank = jnp.sum(jnp.where(before, 1.0, 0.0), axis=0, keepdims=True)
    begin = jnp.sum(jnp.where(key_col < base, 1.0, 0.0), axis=0, keepdims=True)
    rank_col = turn(rank)
    perm = jnp.where(rank_col == col_f, 1.0, 0.0).astype(BF)

    def sort(values):
        total = None
        for part in split3(values):
            term = mm(part, perm)
            total = term if total is None else total + term
        return total

    weight = jnp.where(live, prec[...], 0.0)
    rest = [weight * depart[...], weight, key, rank - begin, jnp.zeros((4, hold), F32)]
    values = [cell.astype(F32), weights[...]] + rest
    ordered = sort(jnp.concatenate(values, axis=0))
    line = iota((8, hold), 0)
    tail = ordered[2 * stencil : 2 * stencil + 8, :]
    first_half = col_f < float(LANES)
    fourfold = 4.0 * jnp.where(first_half, col_f, col_f - float(LANES))
    for i, (low, high) in enumerate(((0.0, 4.0), (1.0, 3.0), (2.0, 2.0))):
        bound = fourfold + jnp.where(first_half, low, high)
        begins = jnp.sum(jnp.where(key_col < bound, 1.0, 0.0), axis=0, keepdims=True)
        tail = jnp.where(line == 5 + i, begins, tail)
    last = (line == 7) & (iota((8, hold), 1) == hold - 1)

    def mark(part, carry):
        low = part * block - margin
        high = (part + 1) * block + margin
        flag = jnp.where(live, any_of((row >= low) & (row < high)), 0.0)
        place = jnp.sum(jnp.where(row_id < col_id, turn(flag), 0.0), axis=0, keepdims=True)
        marks[pl.ds(part, 1), :] = flag * (place + 1.0)
        return carry

    lax.fori_loop(0, parts, mark, 0, unroll=parts <= GROUP)
    listed = marks[...]
    amounts = jnp.max(listed, axis=1, keepdims=True)
    listed = mm(listed.astype(BF), perm)
    for part in range(parts):
        out[part, 0 : 2 * stencil, :] = ordered[0 : 2 * stencil, :]
        out[part, 2 * stencil : 2 * stencil + 8, :] = jnp.where(
            line == 4,
            listed[part : part + 1, :],
            jnp.where(last, amounts[part : part + 1, :], tail),
        )


class Layout:
    def __init__(self, senders, hold, stencil, parts):
        lines = hold // LANES
        self.table = 3 * hold
        sizes = dict(
            addr=stencil * lines, rows=stencil * lines, listed=lines, slot=lines, start=3 * lines
        )
        self.ints = {}
        at = 0
        for name, size in sizes.items():
            self.ints[name] = (at, size)
            at += senders * size
        self.int_rows = at
        self.floats = {}
        at = 0
        for name, size in dict(wgt=stencil * lines, val=lines).items():
            self.floats[name] = (at, size)
            at += senders * size
        self.float_rows = at


def right(x, by):
    return lax.shift_right_logical(x, jnp.full(x.shape, by, I32))


def nt(a, b):
    return lax.dot_general(a, b, (((1,), (1,)), ((), ())), preferred_element_type=F32)


class Received:
    def __init__(self, recv, sender, me, *, parts, columns, height, capacity, stencil):
        senders, _, hold = recv.shape
        wide = columns + 2 * HALO
        block = height // parts
        high_rows = block + 2 * PAD
        cell = recv[sender, 0:stencil, :].astype(I32)
        self.tail = recv[sender, 2 * stencil : 2 * stencil + 8, :]
        self.whole = self.tail.astype(I32)
        self.pos = self.whole[3:4, :]
        owner = right(self.whole[2:3, :], 2)
        offset = owner - me
        offset = jnp.where(offset > parts // 2, offset - parts, offset)
        offset = jnp.where(offset < -(parts // 2), offset + parts, offset)
        column = right(cell, height.bit_length() - 1)
        row = cell & (height - 1)
        at = offset * columns + column + HALO
        self.addr = jnp.where(
            (at >= 0) & (at < wide),
            (right(row, 7) * wide + at) * LANES + (row & (LANES - 1)),
            (height // LANES) * wide * LANES,
        )
        at_row = row - (block * me - PAD)
        across = owner * columns + column
        self.rows = jnp.where(
            (at_row >= 0) & (at_row < high_rows) & (owner < parts),
            (right(across, 7) * high_rows + at_row) * LANES + (across & (LANES - 1)),
            (columns * parts // LANES) * high_rows * LANES,
        )
        self.owner = jnp.minimum(owner, parts - 1)
        self.back = self.owner * (senders * capacity) + sender * capacity + self.pos


def stack_of(addr, weights, tail, back):
    hold = addr.shape[1]
    rows = [
        (addr & (LANES - 1)).astype(F32),
        weights,
        tail,
        right(addr, 7).astype(F32),
        back.astype(F32),
        jnp.zeros((7, hold), F32),
    ]
    return jnp.concatenate(split3(jnp.concatenate(rows, axis=0)), axis=1)


def gathered(stack, chosen):
    select = jnp.where(chosen, 1.0, 0.0).astype(BF)
    return nt(stack, jnp.concatenate([select] * 3, axis=1))


def merge_lines(block, nowhere, stencil, extra):
    number = iota((stencil, LANES), 0).astype(F32)
    line = block[CODES : CODES + stencil, :]
    leader = jnp.zeros(line.shape, F32)
    for k in reversed(range(stencil)):
        leader = jnp.where(line == line[k : k + 1, :], float(k), leader)
    leads = jnp.where(leader == number, 1.0, 0.0)
    count = jnp.zeros((1, LANES), F32)
    ranks = []
    for k in range(stencil):
        ranks.append(count)
        count = count + leads[k : k + 1, :]
    place = jnp.zeros(line.shape, F32)
    for k in range(stencil):
        place = jnp.where(leader == float(k), ranks[k], place)
    lists = []
    for k in range(stencil):
        found = jnp.where((leads > 0.0) & (place == float(k)), line, 0.0)
        found = jnp.sum(found, axis=0, keepdims=True)
        lists.append(jnp.where(count > float(k), found, nowhere))
    batches = right(count.astype(I32) + (BATCH - 1), BATCH.bit_length() - 1)
    most = jnp.zeros((1, LANES), F32)
    slot = iota((1, LANES), 1)
    for begin in range(0, LANES, BLOCK):
        here = (slot >= begin) & (slot < begin + BLOCK)
        found = jnp.max(jnp.where(here, batches.astype(F32), 0.0), axis=1, keepdims=True)
        most = jnp.where(here, found, most)
    back = block[CODES + stencil : CODES + stencil + 1, :]
    ints = [jnp.concatenate(lists, axis=0).astype(I32), batches]
    ints += [most.astype(I32), back.astype(I32)] + extra
    ints = jnp.concatenate(ints, axis=0)
    ints = jnp.concatenate([ints, jnp.zeros((stencil + 8 - ints.shape[0], LANES), I32)], axis=0)
    rows = [
        block[0:CODES, :],
        place * float(LANES) + block[0:stencil, :],
        jnp.zeros((LANES - CODES - stencil, LANES), F32),
    ]
    return ints, jnp.concatenate(rows, axis=0).T


def unpack_kernel(
    meta, recv, _, ints, floats, own_lines, own, total, *, layout, group, **sizes
):
    senders, _, hold = recv.shape
    lines = hold // LANES
    me = meta[0]
    parts, stencil, capacity = sizes["parts"], sizes["stencil"], sizes["capacity"]
    wide = sizes["columns"] + 2 * HALO
    slots = senders * capacity

    def put(ref, place, sender, value):
        begin, size = place
        count = value.shape[0]
        for i in range(lines):
            part = value[:, i * LANES : (i + 1) * LANES]
            if count % 8 == 0:
                at = pl.multiple_of(begin + sender * size + i * count, 8)
                ref[pl.ds(at, count), :] = part
            else:
                for j in range(count):
                    ref[pl.ds(begin + sender * size + i + j * lines, 1), :] = part[j : j + 1]

    total[...] = jnp.zeros(total.shape, F32)
    place = iota((LANES, hold), 0)
    index = iota((LANES, hold), 1)
    lane = iota((1, LANES), 1)
    halo_block = slots // LANES
    after = lax.rem(me + 1, parts)
    ahead = lax.rem(me + parts - 1, parts)

    def per_sender(sender, carry):
        halo_before, amounts = carry
        got = Received(recv, sender, me, **sizes)
        weights = recv[sender, stencil : 2 * stencil, :]
        within = lax.rem(sender, group) * capacity + got.pos
        put(ints, layout.ints["addr"], sender, got.addr)
        put(ints, layout.ints["rows"], sender, got.rows)
        put(ints, layout.ints["listed"], sender, got.whole[4:5, :])
        put(ints, layout.ints["slot"], sender, got.owner * (group * capacity) + within)
        put(ints, layout.ints["start"], sender, got.whole[5:8, :])
        put(floats, layout.floats["wgt"], sender, weights)
        put(floats, layout.floats["val"], sender, got.tail[0:1, :])

        def bound(line, half, owner):
            part = got.whole[5 + line : 6 + line, half * LANES : (half + 1) * LANES]
            return jnp.sum(jnp.where(lane == owner, part, 0), axis=1, keepdims=True)

        stack = stack_of(got.addr, weights, got.tail, got.back)

        begin, end = bound(0, 0, me), bound(0, 1, me)
        first_slot = sender * capacity
        block_of = first_slot // LANES
        within = place - (first_slot - block_of * LANES)
        chosen = (within >= 0) & (index == begin + within) & (index < end)
        shift = first_slot - block_of * LANES
        here = (lane >= shift) & (lane < shift + (end - begin))
        total[block_of] = jnp.where(here, gathered(stack, chosen), total[block_of])
        amounts = jnp.where(lane == sender, end - begin, amounts)

        first_r, last_r = bound(1, 0, after), bound(1, 1, after)
        first_l, last_l = bound(2, 0, ahead), bound(0, 1, ahead)
        middle = halo_before + (last_r - first_r)
        chosen_r = (index >= first_r) & (index < last_r) & (index - first_r + halo_before == place)
        chosen_l = (index >= first_l) & (index < last_l) & (index - first_l + middle == place)
        halo_after = middle + (last_l - first_l)
        here = (lane >= halo_before) & (lane < halo_after)
        values = gathered(stack, chosen_r | chosen_l)
        total[halo_block] = jnp.where(here, values, total[halo_block])
        return halo_after, amounts

    halo_count, amounts = lax.fori_loop(
        0,
        senders,
        per_sender,
        (jnp.zeros((1, 1), I32), jnp.zeros((1, LANES), I32)),
        unroll=senders <= GROUP,
    )
    extra = [amounts, jnp.broadcast_to(halo_count, (1, LANES))]
    nowhere = float((sizes["height"] // LANES) * wide)
    for i in range(slots // LANES + 1):
        top = i * (stencil + 8)
        own_lines[top : top + stencil + 8, :], own[i * LANES : (i + 1) * LANES, :] = merge_lines(
            total[i], nowhere, stencil, extra
        )


def list_kernel(meta, recv, _, row_lines, row_data, total, **sizes):
    senders, _, hold = recv.shape
    stencil = sizes["stencil"]
    high_rows = sizes["height"] // sizes["parts"] + 2 * PAD
    place = iota((LISTED, hold), 0)
    total[...] = jnp.zeros(total.shape, F32)

    def per_sender(sender, before):
        got = Received(recv, sender, meta[0], **sizes)
        marks = got.whole[4:5, :]
        zeros = jnp.zeros((stencil, hold), F32)
        tail = jnp.concatenate([got.tail[0:1, :], zeros[0:7, :]], axis=0)
        stack = stack_of(got.rows, zeros, tail, got.back)
        values = gathered(stack, (marks > 0) & (marks - 1 + before == place))
        after = before + got.whole[7:8, hold - 1 : hold]
        slot = iota((1, LISTED), 1)
        total[...] = jnp.where((slot >= before) & (slot < after), values, total[...])
        return after

    count = lax.fori_loop(
        0, senders, per_sender, jnp.zeros((1, 1), I32), unroll=senders <= GROUP
    )
    nowhere = float((sizes["columns"] * sizes["parts"] // LANES) * high_rows)
    for i in range(LISTED // LANES):
        top = i * (stencil + 8)
        block = total[:, i * LANES : (i + 1) * LANES]
        (
            row_lines[top : top + stencil + 8, :],
            row_data[i * LANES : (i + 1) * LANES, :],
        ) = merge_lines(block, nowhere, stencil, [jnp.broadcast_to(count, (1, LANES))])


class RowCopies:
    def __init__(self, source, target, room, table, sems, stencil):
        half = 2 * BATCH * room
        self.always = pltpu.make_async_copy(
            source.at[pl.ds(0, half), :], target.at[pl.ds(0, half), :], sems[0]
        )
        size = source.shape[0] - half
        self.seldom = pltpu.make_async_copy(
            source.at[pl.ds(half, size), :], target.at[pl.ds(half, size), :], sems[1]
        )
        self.table, self.room, self.stencil = table, room, stencil

    def rest(self):
        most = word_of(self.table, 0, self.stencil + 1, self.stencil)
        for top in range(BLOCK, self.room, BLOCK):
            most = jnp.maximum(most, word_of(self.table, top, self.stencil + 1, self.stencil))
        return most > 2

    def run_rest(self):
        @pl.when(self.rest())
        def _():
            self.seldom.start()
            self.seldom.wait()


def word_of(table, slot, k, stencil):
    at = lax.shift_right_logical(slot, 7) * ((stencil + 7) * LANES) + slot
    return table[at + k * LANES]


def columns_of(info, begin, stencil):
    return [jnp.broadcast_to(info[:, begin + k : begin + k + 1], info.shape) for k in range(stencil)]


def weight_rows(info, places, stencil):
    lane_f = iota(info.shape, 1).astype(F32)
    codes = columns_of(info, CODES, stencil)
    weights = columns_of(info, stencil, stencil)
    rows = []
    for place in range(stencil):
        row = jnp.zeros(info.shape, F32)
        if place < places:
            at = lane_f + float(LANES * place)
            for k in range(place, stencil):
                term = jnp.where(at == codes[k], weights[k], 0.0)
                row = term if k == place else row + term
        rows.append(row)
    return rows


def block_at(table, top, stencil, action):
    top = pl.multiple_of(top, 8)
    most = word_of(table, top, stencil + 1, stencil)

    @pl.when(most <= 1)
    def _():
        action(top, BATCH)

    @pl.when(most == 2)
    def _():
        action(top, 2 * BATCH)

    @pl.when(most > 2)
    def _():
        action(top, stencil)


def blocks_of(table, top, amount, stencil, action):
    def step(i, carry):
        block_at(table, top + i * BLOCK, stencil, action)
        return carry

    lax.fori_loop(0, lax.div(amount + (BLOCK - 1), BLOCK), step, 0)


def factor_kernel(
    lines_h, data, replies, _, merged_h, mixed, lines_s, table, merged, sems, *, stencil, slots
):
    parts = replies.shape[0]
    lines = slots // LANES
    lines_copy = pltpu.make_async_copy(lines_h, lines_s, sems.at[0])
    lines_copy.start()

    def per_owner(owner, carry):
        for i in range(lines):
            rows = [
                jnp.zeros((stencil, LANES), F32),
                replies[owner, pl.ds(8 + i, stencil, stride=lines), :],
                jnp.zeros((1, LANES), F32),
                replies[owner, i : i + 1, :],
                jnp.zeros((LANES - 2 * stencil - 2, LANES), F32),
            ]
            at = pl.multiple_of(owner * slots + i * LANES, LANES)
            table[pl.ds(at, LANES), :] = jnp.concatenate(rows, axis=0).T
        return carry

    lax.fori_loop(0, parts, per_owner, 0, unroll=parts <= GROUP)
    lines_copy.wait()
    count = jnp.minimum(lines_s[(stencil + 3) * LANES], LISTED)

    def mix(numbers, weights):
        for slot in numbers:
            back = word_of(lines_s, slot, stencil + 2, stencil)
            mixed[pl.ds(slot, 1), :] = data[pl.ds(slot, 1), :] + table[pl.ds(back, 1), :]

    quads(0, count, mix)

    def build(top, places):
        rows = weight_rows(mixed[pl.ds(top, BLOCK), :], places, stencil)
        for place, row in enumerate(rows):
            merged[pl.ds(place * LISTED + top, BLOCK), :] = row

    blocks_of(lines_s, 0, count, stencil, build)
    copies = RowCopies(
        merged, merged_h, LISTED, lines_s, (sems.at[1], sems.at[2]), stencil
    )
    copies.always.start()
    copies.run_rest()
    copies.always.wait()


def most_batches(table, slots, stencil):
    most = word_of(table, slots[0], stencil, stencil)
    for slot in slots[1:]:
        most = jnp.maximum(most, word_of(table, slot, stencil, stencil))
    return most


def scatter_slots(table, merged, room, copies, slots, values, stencil):
    def batch(begin):
        for first in range(0, len(slots), len(copies)):
            todo = []
            some = slice(first, first + len(copies))
            for slot, value, ref in zip(slots[some], values[some], copies):
                for j in range(BATCH):
                    line = word_of(table, slot, begin + j, stencil)
                    row = merged[pl.ds((begin + j) * room + slot, 1), :] * value
                    todo.append((ref, line, ref[pl.ds(line, 1), :] + row))
            for ref, line, row in todo:
                ref[pl.ds(line, 1), :] = row

    def more(i, carry):
        batch(i * BATCH)
        return carry

    batch(0)
    lax.fori_loop(1, most_batches(table, slots, stencil), more, 0)


def band(shape, taps, shift):
    distance = iota(shape, 1) - iota(shape, 0) + shift
    result = jnp.zeros(shape, F32)
    for tap in range(taps.shape[0]):
        result = jnp.where(distance == tap, taps[tap], result)
    return result


def band_rev(shape, taps, shift):
    distance = iota(shape, 0) - iota(shape, 1) + shift
    result = jnp.zeros(shape, F32)
    for tap in range(taps.shape[0]):
        result = jnp.where(distance == tap, taps[tap], result)
    return result


def exact_nt(a, b):
    return lax.dot_general(
        a,
        b,
        (((1,), (1,)), ((), ())),
        precision=lax.Precision.HIGHEST,
        preferred_element_type=F32,
    )


def store_split(ref, index, value):
    high, low = split2(value)
    ref[(0,) + index] = high
    ref[(1,) + index] = low


def bands_kernel(kx, ky, lat2, lon2, lat1, lon1, *, rows_block):
    margin = kx.shape[0] // 2
    window = lat2.shape[2]
    first = band((window, window), ky, margin)
    reach = first[LANES : LANES + WIDE, :]
    place = iota((window, window), 1)
    for variant in range(3):
        kept = first
        if variant == 0:
            kept = jnp.where(place >= LANES, first, 0.0)
        if variant == 2:
            kept = jnp.where(place < LANES + WIDE, first, 0.0)
        store_split(lat2, (variant,), exact_nt(kept, reach))
    size = lon2.shape[1]
    wide = size + 2 * HALO
    depth = (wide + 32 + LANES - 1) // LANES * LANES
    second = band((wide, depth), kx, -(16 - margin))
    store_split(lon2, (), exact_nt(second[HALO : HALO + size, :], second))
    store_split(lat1, (), band_rev((rows_block, rows_block + 2 * PAD), ky, PAD + margin))
    store_split(lon1, (), band((2 * WIDE, WIDE), kx, LANES + margin))


def pairs(low, high, action):
    def step(i, carry):
        one = low + 2 * i
        action(one, jnp.minimum(one + 1, high - 1), one + 1 < high)
        return carry

    lax.fori_loop(0, lax.shift_right_logical(high - low + 1, 1), step, 0)


def quads(low, high, action):
    def step(i, carry):
        one = low + 4 * i
        numbers = [one] + [jnp.minimum(one + j, high - 1) for j in range(1, 4)]
        weights = [None] + [jnp.where(one + j < high, 1.0, 0.0) for j in range(1, 4)]
        action(numbers, weights)
        return carry

    lax.fori_loop(0, lax.shift_right_logical(high - low + 3, 2), step, 0)


def weighted(value, weight):
    return value if weight is None else value * weight


def zero_all(refs):
    rows = refs[0].shape[0]
    step = 256

    def clear(i, carry):
        for ref in refs:
            ref[pl.ds(pl.multiple_of(i * step, 8), step), :] = jnp.zeros((step, LANES), F32)
        return carry

    whole = rows // step
    lax.fori_loop(0, whole, clear, 0)
    if rows % step:
        for ref in refs:
            ref[whole * step : rows, :] = jnp.zeros((rows % step, LANES), F32)


def scatter_entries(copies, entries, lane):
    for start in range(0, len(entries), len(copies)):
        group = []
        for ref, (address, value) in zip(copies, entries[start : start + len(copies)]):
            line = lax.shift_right_logical(address, 7)
            spread = jnp.where(lane == (address & (LANES - 1)), value, 0.0)
            group.append((ref, line, ref[pl.ds(line, 1), :] + spread))
        for ref, line, value in group:
            ref[pl.ds(line, 1), :] = value


def spot(sender, idx, per, stencil):
    return sender * per + idx + lax.shift_right_logical(idx, 7) * ((stencil - 1) * LANES)


def copy_parts(layout, source, target, place, chunk, chunks, group, sem):
    begin, size = place
    words = group * size * LANES
    at = begin * LANES + chunk * words
    return pltpu.make_async_copy(source.at[pl.ds(at, words)], target, sem)


def apply_kernel(
    *refs, first, layout, columns, height, hold, stencil, capacity, senders, parts, levels
):
    refs = list(refs)

    def take(count):
        taken = refs[:count]
        del refs[:count]
        return taken

    meta, ints, floats, own_lines, own = take(5)
    if not first:
        replies_h, replies = take(2)
    std_h, std_l_h, std_r_h, lat2_h, lon2_h = take(5)
    if not first:
        merged_h, _ = take(2)
    field_h, send = take(2)
    if first:
        info_out, merged_h = take(2)
    addr, wgt, start, lines_s, val = take(5)
    if first:
        std_flat, picked, chosen = take(3)
    scale, merged, sums, high_s, low_s, std, std_l, std_r, lat2, lon2, field = take(11)
    copies = take(PAIR)
    sems, in_sems, out_sems, val_sem = take(4)

    me = meta[0]
    wide = columns + 2 * HALO
    blocks = height // LANES
    group = min(GROUP, senders)
    chunks = senders // group
    slots = senders * capacity
    lane = iota((1, LANES), 1)
    per = stencil * hold
    table = layout.table

    def chunk_copies(chunk):
        todo = [
            (ints, addr, layout.ints["addr"]),
            (floats, wgt, layout.floats["wgt"]),
            (ints, start, layout.ints["start"]),
        ]
        if first:
            todo.append((floats, val, layout.floats["val"]))
        return [
            copy_parts(layout, source, target, place, chunk, chunks, group, sems.at[i])
            for i, (source, target, place) in enumerate(todo)
        ]

    def load_chunk(chunk):
        for copy in chunk_copies(chunk):
            copy.start()
        for copy in chunk_copies(chunk):
            copy.wait()

    operands = [
        pltpu.make_async_copy(source, target, in_sems.at[i])
        for i, (source, target) in enumerate(
            (
                (std_h, std),
                (std_l_h, std_l),
                (std_r_h, std_r),
                (lat2_h, lat2),
                (lon2_h, lon2),
            )
        )
    ]
    own_copy = pltpu.make_async_copy(own_lines, lines_s, in_sems.at[5])
    own_copy.start()
    merged_copies = RowCopies(
        *((merged, merged_h) if first else (merged_h, merged)),
        slots + LANES,
        lines_s,
        (in_sems.at[6], in_sems.at[7]),
        stencil,
    )
    if not first:
        merged_copies.always.start()
    for copy in operands:
        copy.start()

    def value_copy(owner):
        at = pl.multiple_of(owner * (replies_h.shape[0] // parts), 1024)
        return pltpu.make_async_copy(
            replies_h.at[pl.ds(at, slots)], val.at[pl.ds(owner * slots, slots)], val_sem.at[owner]
        )

    def each_owner(action):
        def step(owner, carry):
            action(value_copy(owner))
            return carry

        lax.fori_loop(0, parts, step, 0)

    if not first:
        each_owner(lambda copy: copy.start())
    zero_all(copies)
    zero_all([sums])

    lane_of = iota((slots, LANES), 1)
    room = slots + LANES
    column = 2 * stencil if first else 2 * stencil + 2
    scale[...] = jnp.broadcast_to(own[:, column : column + 1], (room, LANES))
    known = own[0:slots, :]
    own_copy.wait()
    if not first:
        merged_copies.always.wait()
        merged_copies.run_rest()

    after = lax.rem(me + 1, parts)
    ahead = lax.rem(me + parts - 1, parts)

    def start_of(sender, owner, row, half):
        return start[sender * table + row * hold + half * LANES + owner]

    def entries_of(sender, idx, value):
        base = spot(sender, idx, per, stencil)
        return [
            (addr[base + k * LANES], wgt[base + k * LANES] * value) for k in range(stencil)
        ]

    def own_line(slot, k):
        return word_of(lines_s, slot, k, stencil)

    def amount_of(sender):
        return lines_s[(stencil + 3) * LANES + sender]

    halo_count = lines_s[(stencil + 4) * LANES]
    halo_fits = halo_count <= LANES

    def own_groups(action, halo):
        if capacity % BLOCK:
            blocks_of(lines_s, 0, slots, stencil, action)
        else:

            def per_sender(sender, carry):
                blocks_of(lines_s, sender * capacity, amount_of(sender), stencil, action)
                return carry

            lax.fori_loop(0, senders, per_sender, 0)
        if halo:
            blocks_of(lines_s, slots, jnp.minimum(halo_count, LANES), stencil, action)

    def build(top, places):
        rows = weight_rows(own[pl.ds(top, BLOCK), :], places, stencil)
        for place, row in enumerate(rows):
            merged[pl.ds(place * room + top, BLOCK), :] = row

    if first:
        own_groups(build, True)
        merged_copies.always.start()
        merged_copies.run_rest()

    def own_quads(action):
        def per_sender(sender, carry):
            base = sender * capacity
            quads(base, base + amount_of(sender), action)
            return carry

        lax.fori_loop(0, senders, per_sender, 0)

    def scatter_known(numbers, weights):
        values = [weighted(scale[pl.ds(i, 1), :], w) for i, w in zip(numbers, weights)]
        scatter_slots(lines_s, merged, room, copies, numbers, values, stencil)

    def scatter_sent(numbers, weights):
        values = [weighted(val[own_line(i, stencil + 2)], w) for i, w in zip(numbers, weights)]
        scatter_slots(lines_s, merged, room, copies, numbers, values, stencil)

    def scatter_halo(chunk):
        def per_sender(sender, carry):
            for owner, low, high in ((after, (1, 0), (1, 1)), (ahead, (2, 0), (0, 1))):
                begin = start_of(sender, owner, 0, 0)

                def value_of(idx, owner=owner, begin=begin):
                    if first:
                        return val[sender * hold + idx]
                    place = (chunk * group + sender) * capacity + idx - begin
                    return val[owner * slots + place]

                def action(one, two, has_two, value_of=value_of):
                    second = jnp.where(has_two, value_of(two), 0.0)
                    scatter_entries(
                        copies,
                        entries_of(sender, one, value_of(one)) + entries_of(sender, two, second),
                        lane,
                    )

                pairs(start_of(sender, owner, *low), start_of(sender, owner, *high), action)
            return carry

        lax.fori_loop(0, group, per_sender, 0)

    own_quads(scatter_known)
    if not first:
        each_owner(lambda copy: copy.wait())

    @pl.when(halo_fits)
    def _():
        quads(slots, slots + halo_count, scatter_known if first else scatter_sent)

    @pl.when(jnp.logical_not(halo_fits))
    def _():
        def step(chunk, carry):
            load_chunk(chunk)
            scatter_halo(chunk)
            return carry

        lax.fori_loop(0, chunks, step, 0)

    for copy in operands:
        copy.wait()

    def prepare(jb):
        lanes = slice(jb * LANES, (jb + 1) * LANES)
        for low, size, source in (
            (0, HALO, std_l),
            (HALO, columns, std),
            (HALO + columns, HALO, std_r),
        ):
            rows = slice(jb * wide + low, jb * wide + low + size)
            total = copies[0][rows, :]
            for ref in copies[1:]:
                total = total + ref[rows, :]
            high, lo = split2(total * source[:, lanes])
            high_s[low : low + size, lanes] = high
            low_s[low : low + size, lanes] = lo
        if first:
            std_flat[jb * wide + HALO : jb * wide + HALO + columns, :] = std[:, lanes]

    smoothed = copies[0]
    size = lon2.shape[1]
    count = height // WIDE
    outgoing = [merged_copies.always] if first else []

    def along_latitude(block):
        variant = 0 if block == 0 else (2 if block == count - 1 else 1)
        low = max(block * WIDE - LANES, 0)
        high = min(block * WIDE + WIDE + LANES, height)
        inner = slice(low - (block * WIDE - LANES), high - (block * WIDE - LANES))
        matrix = (lat2[0, variant, inner, :], lat2[1, variant, inner, :])
        return split2(mm_parts((high_s[:, low:high], low_s[:, low:high]), matrix))

    def along_longitude(block, parts_y):
        lanes = slice(block * WIDE, (block + 1) * WIDE)
        for begin in range(0, columns, size):
            some = min(size, columns - begin)
            rows = slice(begin, begin + some)
            window = slice(begin, begin + some + 2 * HALO)
            matrix = tuple(lon2[i, 0:some, 0 : some + 2 * HALO] for i in range(2))
            result = mm_parts(matrix, (parts_y[0][window, :], parts_y[1][window, :]))
            scaled = result * std[rows, lanes]
            field[rows, lanes] = scaled
            for half in range(WIDE // LANES):
                top = (block * (WIDE // LANES) + half) * wide + HALO + begin
                smoothed[top : top + some, :] = scaled[:, half * LANES : (half + 1) * LANES]
        outgoing.append(
            pltpu.make_async_copy(field.at[:, lanes], field_h.at[:, lanes], out_sems.at[block])
        )
        outgoing[-1].start()

    ready = 0
    waiting = None
    for block in range(count + 1):
        upto = min((block + 1) * (WIDE // LANES) + 1, blocks)
        for jb in range(ready, upto):
            prepare(jb)
        ready = max(ready, upto)
        following = along_latitude(block) if block < count else None
        if block > 0:
            along_longitude(block - 1, waiting)
        waiting = following

    def gather_quad(numbers, weights):
        def batch(begin, totals):
            result = []
            for slot, total in zip(numbers, totals):
                terms = []
                for j in range(BATCH):
                    line = own_line(slot, begin + j)
                    row = merged[pl.ds((begin + j) * room + slot, 1), :]
                    terms.append(row * smoothed[pl.ds(line, 1), :])
                    if first:
                        picked[pl.ds((begin + j) * room + slot, 1), :] = std_flat[
                            pl.ds(line, 1), :
                        ]
                result.append(total + ((terms[0] + terms[1]) + (terms[2] + terms[3])))
            return tuple(result)

        zero = jnp.zeros((1, LANES), F32)
        totals = lax.fori_loop(
            1,
            most_batches(lines_s, numbers, stencil),
            lambda i, totals: batch(i * BATCH, totals),
            batch(0, (zero,) * len(numbers)),
        )
        for slot, total in zip(numbers, totals):
            sums[pl.ds(slot, 1), :] = total

    own_quads(gather_quad)

    def pick(top, places):
        info = own[pl.ds(top, BLOCK), :]
        codes = columns_of(info, CODES, stencil)
        lane_f = iota(info.shape, 1).astype(F32)
        rows = [picked[pl.ds(place * room + top, BLOCK), :] for place in range(places)]
        result = jnp.zeros((BLOCK, LANES), F32)
        for k in range(stencil):
            cell = jnp.zeros((BLOCK, LANES), F32)
            for place in range(min(k + 1, places)):
                at = lane_f + float(LANES * place)
                cell = jnp.where(at == codes[k], rows[place], cell)
            cell = jnp.sum(cell, axis=1, keepdims=True)
            result = jnp.where(lane_f == float(stencil + k), cell, result)
        chosen[pl.ds(top, BLOCK), :] = result * info

    if first:
        own_groups(pick, False)

    def whole(x):
        return jnp.sum(x, axis=0, keepdims=True)

    total = jnp.sum(sums[...], axis=1, keepdims=True)
    lines = slots // LANES
    known = own[0:slots, :]
    source, weight, reply, image0 = (
        known[:, 2 * stencil + i : 2 * stencil + i + 1] for i in range(4)
    )
    if first:
        reply = weight * total
        known = jnp.where(lane_of == 2 * stencil + 2, reply, known)
        known = jnp.where(lane_of == 2 * stencil + 3, total, known)
        info_out[0:slots, :] = known
        info_out[slots:room, :] = own[slots:room, :]
        turned = known.T[2 * stencil + 2 : 2 * stencil + 3, :]
        message = [turned[:, i * LANES : (i + 1) * LANES] for i in range(lines)]
        message.append(
            jnp.where(
                lane == 0, whole(source * total), jnp.where(lane == 1, whole(reply * total), 0.0)
            )
        )
        message.append(jnp.zeros((8 - len(message), LANES), F32))
        factors = chosen[...].T
        for k in range(stencil):
            row = factors[stencil + k : stencil + k + 1, :]
            message += [row[:, i * LANES : (i + 1) * LANES] for i in range(lines)]
        message = jnp.concatenate(message, axis=0)
    else:
        slab = jnp.sum(replies[:, 0:8, :], axis=0)[lines : lines + 1, :]
        length = slab[:, 0:1] / (slab[:, 0:1] + slab[:, 1:2])
        both = source + reply
        s_both = image0 + total
        resid = source - length * both
        s_resid = image0 - length * s_both
        values = [
            resid * s_resid,
            resid * s_both,
            both * s_both,
            resid * image0,
            both * image0,
            weight * s_resid * s_resid,
            weight * s_resid * s_both,
            weight * s_both * s_both,
            weight * s_resid * image0,
            weight * s_both * image0,
            source * image0,
            reply * image0,
        ]
        message = jnp.where(lane == len(values), length, 0.0)
        for i, value in enumerate(values):
            message = jnp.where(lane == i, whole(value), message)
        message = jnp.concatenate([message, jnp.zeros((7, LANES), F32)], axis=0)

    def send_to(i, carry):
        send[i] = message
        return carry

    lax.fori_loop(0, send.shape[0], send_to, 0)
    for copy in outgoing:
        copy.wait()


def final_kernel(
    ints,
    floats,
    replies_h,
    lines_h,
    merged_h,
    mixed,
    totals,
    field0_h,
    field1_h,
    lat1,
    lon1,
    control_h,
    increment_h,
    addr,
    listed,
    slot,
    val,
    factors,
    field0,
    field1,
    control,
    high_s,
    low_s,
    lines_s,
    merged,
    scale,
    *rest,
    layout,
    hold,
    stencil,
    capacity,
    senders,
    parts,
    length,
):
    copies = rest[:PAIR]
    sems, in_sems, out_sems = rest[PAIR:]
    group = min(GROUP, senders)
    chunks = senders // group
    per = stencil * hold
    rows_block = control.shape[0]
    high_rows = rows_block + 2 * PAD
    lane = iota((1, LANES), 1)
    stride = group * capacity
    owner_words = factors.shape[0] // parts
    to_factors = owner_words - stencil * stride

    def chunk_copies(chunk):
        todo = [
            (ints, addr, layout.ints["rows"]),
            (ints, listed, layout.ints["listed"]),
            (ints, slot, layout.ints["slot"]),
            (floats, val, layout.floats["val"]),
        ]
        result = [
            copy_parts(layout, source, target, place, chunk, chunks, group, sems.at[i])
            for i, (source, target, place) in enumerate(todo)
        ]
        words = parts * owner_words
        result.append(
            pltpu.make_async_copy(
                replies_h.at[pl.ds(chunk * words, words)], factors, sems.at[len(todo)]
            )
        )
        return result

    row_copies = RowCopies(
        merged_h, merged, LISTED, lines_s, (in_sems.at[3], in_sems.at[4]), stencil
    )
    listing = [pltpu.make_async_copy(lines_h, lines_s, in_sems.at[2]), row_copies.always]
    for copy in listing:
        copy.start()
    operands = [
        pltpu.make_async_copy(source, target, in_sems.at[i])
        for i, (source, target) in enumerate(
            ((field0_h, field0), (field1_h, field1))
        )
    ]
    for copy in operands:
        copy.start()

    slabs = totals.shape[1]
    every = jnp.sum(totals[...], axis=0)
    norm0 = quad0 = None
    for i in range(slabs):
        line = every[i, 0:1, :]
        a, b = line[:, 10:11], line[:, 11:12]
        norm0 = a if norm0 is None else norm0 + a
        quad0 = b if quad0 is None else quad0 + b
    step0 = norm0 / (norm0 + quad0)
    norm1 = cross = quad1 = quad01 = jnp.zeros((1, 1), F32)
    for i in range(slabs):
        line = every[i, 0:1, :]
        v = [line[:, j : j + 1] for j in range(10)]
        shift = totals[0, i, 0:1, 12:13] - step0
        norm1 = norm1 + (v[0] + shift * (2.0 * v[1] + shift * v[2]))
        cross = cross + (v[3] + shift * v[4])
        quad1 = quad1 + (v[5] + shift * (2.0 * v[6] + shift * v[7]))
        quad01 = quad01 + (v[8] + shift * v[9])
    ratio = norm1 / norm0
    curvature = norm1 + quad1 + ratio * (
        2.0 * (cross + quad01) + ratio * (norm0 + quad0)
    )
    step1 = norm1 / curvature
    first = step0 + step1 * (1.0 - step0 + ratio)
    second = -step0 * step1
    first_line = jnp.broadcast_to(first, (1, LANES))
    second_line = jnp.broadcast_to(second, (1, LANES))

    zero_all(copies)

    data = mixed[...]
    column = 2 * stencil
    scale[...] = first * data[:, column : column + 1] + second * jnp.broadcast_to(
        data[:, column + 1 : column + 2], data.shape
    )
    for copy in listing:
        copy.wait()
    row_copies.run_rest()
    count = lines_s[(stencil + 3) * LANES]

    def add(numbers, weights):
        values = [weighted(scale[pl.ds(i, 1), :], w) for i, w in zip(numbers, weights)]
        scatter_slots(lines_s, merged, LISTED, copies, numbers, values, stencil)

    def scatter_chunk():
        def per_sender(sender, carry):
            def step(idx, inner):
                @pl.when(listed[sender * hold + idx] > 0)
                def _():
                    place = slot[sender * hold + idx]
                    place = place + lax.div(place, stride) * (owner_words - stride)
                    base = spot(sender, idx, per, stencil)
                    z0 = val[sender * hold + idx]
                    value = first_line * z0 + second_line * factors[place]
                    entries = [
                        (addr[base + k * LANES], factors[place + to_factors + k * stride] * value)
                        for k in range(stencil)
                    ]
                    scatter_entries(copies, entries, lane)

                return inner

            lax.fori_loop(0, hold, step, 0)
            return carry

        lax.fori_loop(0, group, per_sender, 0)

    @pl.when(count <= LISTED)
    def _():
        quads(0, count, add)

    @pl.when(count > LISTED)
    def _():
        def step(chunk, carry):
            for copy in chunk_copies(chunk):
                copy.start()
            for copy in chunk_copies(chunk):
                copy.wait()
            scatter_chunk()
            return carry

        lax.fori_loop(0, chunks, step, 0)

    for copy in operands:
        copy.wait()
    increment = field0
    increment[...] = first * field0[...] + second * field1[...]
    outgoing = [pltpu.make_async_copy(increment, increment_h, out_sems.at[0])]
    outgoing[0].start()

    pair = WIDE // LANES
    count = length // WIDE

    def along_latitude(block):
        pieces = []
        for half in range(pair):
            rows = slice((block * pair + half) * high_rows, (block * pair + half + 1) * high_rows)
            total = copies[0][rows, :]
            for ref in copies[1:]:
                total = total + ref[rows, :]
            pieces.append(total)
        whole = split2(jnp.concatenate(pieces, axis=1))
        size = lat1.shape[1]
        for top in range(0, rows_block, size):
            window = slice(top, top + size + 2 * PAD)
            along = mm_parts((lat1[0], lat1[1]), (whole[0][window, :], whole[1][window, :]))
            high, low = split2(along)
            high_s[top : top + size, block * WIDE : (block + 1) * WIDE] = high
            low_s[top : top + size, block * WIDE : (block + 1) * WIDE] = low

    def window(ref, block):
        low, high = block * WIDE - LANES, (block + 1) * WIDE + LANES
        if low < 0:
            return jnp.concatenate([ref[:, length + low : length], ref[:, 0:high]], axis=1)
        if high > length:
            return jnp.concatenate([ref[:, low:length], ref[:, 0 : high - length]], axis=1)
        return ref[:, low:high]

    every_lanes = 4

    def along_longitude(block):
        control[:, block * WIDE : (block + 1) * WIDE] = mm_parts(
            (window(high_s, block), window(low_s, block)), (lon1[0], lon1[1])
        )
        if block % every_lanes == every_lanes - 1:
            lanes = slice((block + 1 - every_lanes) * WIDE, (block + 1) * WIDE)
            outgoing.append(
                pltpu.make_async_copy(
                    control.at[:, lanes], control_h.at[:, lanes], out_sems.at[len(outgoing)]
                )
            )
            outgoing[-1].start()

    along_latitude(count - 1)
    along_latitude(0)
    along_latitude(1)
    for block in range(count):
        if 2 <= block + 2 < count - 1:
            along_latitude(block + 2)
        along_longitude(block)
    for copy in outgoing:
        copy.wait()


def body(
    background_std,
    x_kernel,
    y_kernel,
    obs_owner,
    obs_cells,
    obs_weights,
    innovation,
    obs_precision,
    obs_counts,
):
    parts = lax.axis_size("pencil")
    levels = lax.axis_size("lev")
    me = lax.axis_index("pencil")
    _, columns, height = background_std.shape
    hold, stencil = obs_cells.shape
    margin = x_kernel.shape[1] // 2
    capacity = 2 * hold // parts
    senders = parts
    slots = senders * capacity
    room = slots + LANES
    rows_block = height // parts
    length = columns * parts
    blocks = height // LANES
    wide = columns + 2 * HALO
    group = min(GROUP, senders)
    chunks = senders // group
    layout = Layout(senders, hold, stencil, parts)
    std = background_std[0]

    packed = pl.pallas_call(
        functools.partial(
            pack_kernel, parts=parts, columns=columns, height=height, margin=margin
        ),
        out_shape=jax.ShapeDtypeStruct((parts, PACK, hold), F32),
        in_specs=[smem()] + [vmem()] * 5,
        out_specs=vmem(),
        scratch_shapes=[pltpu.VMEM((parts, hold), F32)],
        compiler_params=params(),
        cost_estimate=cost(12000),
        name="pack",
    )(
        obs_counts,
        obs_owner.T,
        obs_cells.T,
        obs_weights.T,
        innovation[None, :],
        obs_precision[None, :],
    )
    recv = lax.all_to_all(packed, "pencil", split_axis=0, concat_axis=0, tiled=True)

    right_of = [(p, (p + 1) % parts) for p in range(parts)]
    left_of = [(p, (p - 1) % parts) for p in range(parts)]
    std_l = lax.ppermute(std[columns - HALO :, :], "pencil", right_of)
    std_r = lax.ppermute(std[:HALO, :], "pencil", left_of)

    size = min(columns, WIDE - 2 * HALO)
    row_size = min(rows_block, LANES)
    lat2, lon2, lat1, lon1 = pl.pallas_call(
        functools.partial(bands_kernel, rows_block=row_size),
        out_shape=[
            jax.ShapeDtypeStruct((2, 3, 2 * WIDE, WIDE), BF),
            jax.ShapeDtypeStruct((2, size, size + 2 * HALO), BF),
            jax.ShapeDtypeStruct((2, row_size, row_size + 2 * PAD), BF),
            jax.ShapeDtypeStruct((2, 2 * WIDE, WIDE), BF),
        ],
        in_specs=[smem(), smem()],
        out_specs=[vmem()] * 4,
        compiler_params=params(),
        cost_estimate=cost(100),
        name="bands",
    )(x_kernel[0], y_kernel[0])

    meta = jnp.reshape(me, (1,)).astype(I32)
    place = dict(
        parts=parts, columns=columns, height=height, capacity=capacity, stencil=stencil
    )
    ints, floats, own_lines, own = pl.pallas_call(
        functools.partial(unpack_kernel, layout=layout, group=group, **place),
        out_shape=[
            jax.ShapeDtypeStruct((layout.int_rows, LANES), I32),
            jax.ShapeDtypeStruct((layout.float_rows, LANES), F32),
            jax.ShapeDtypeStruct((room // LANES * (stencil + 8), LANES), I32),
            jax.ShapeDtypeStruct((room, LANES), F32),
        ],
        in_specs=[smem(), vmem(), hbm()],
        out_specs=[vmem()] * 4,
        scratch_shapes=[
            pltpu.VMEM((room // LANES, STACK, LANES), F32),
        ],
        compiler_params=params(),
        cost_estimate=cost(100),
        name="unpack",
    )(meta, recv, lat1)
    ints = ints.reshape(-1)
    floats = floats.reshape(-1)
    own_lines = own_lines.reshape(-1)

    acc = pltpu.VMEM((blocks * wide + 8, LANES), F32)
    column_slots = pltpu.VMEM((slots, LANES), F32)
    static = dict(
        layout=layout,
        columns=columns,
        height=height,
        hold=hold,
        stencil=stencil,
        capacity=capacity,
        senders=senders,
        parts=parts,
        levels=levels,
    )
    per = group * stencil * hold
    line = group * hold
    index_scratch = [
        pltpu.SMEM((per,), I32),
        pltpu.SMEM((per,), F32),
        pltpu.SMEM((group * layout.table,), I32),
        pltpu.SMEM((room * (stencil + 8),), I32),
    ]
    work = (
        [
            pltpu.VMEM((room, LANES), F32),
            pltpu.VMEM((stencil * room, LANES), F32),
            column_slots,
        ]
        + [pltpu.VMEM((wide, height), BF)] * 2
        + [
            pltpu.VMEM((columns, height), F32),
            pltpu.VMEM((HALO, height), F32),
            pltpu.VMEM((HALO, height), F32),
            pltpu.VMEM(lat2.shape, BF),
            pltpu.VMEM(lon2.shape, BF),
            pltpu.VMEM((columns, height), F32),
        ]
        + [acc] * PAIR
        + [
            pltpu.SemaphoreType.DMA((4,)),
            pltpu.SemaphoreType.DMA((8,)),
            pltpu.SemaphoreType.DMA((height // WIDE,)),
            pltpu.SemaphoreType.DMA((parts,)),
        ]
    )
    field_shape = jax.ShapeDtypeStruct((columns, height), F32)
    reply_rows = 8 + stencil * slots // LANES
    field0, message, info, merged = pl.pallas_call(
        functools.partial(apply_kernel, first=True, **static),
        out_shape=[
            field_shape,
            jax.ShapeDtypeStruct((parts, reply_rows, LANES), F32),
            jax.ShapeDtypeStruct((room, LANES), F32),
            jax.ShapeDtypeStruct((stencil * room, LANES), F32),
        ],
        in_specs=[smem()] + [hbm()] * 3 + [vmem()] + [hbm()] * 5,
        out_specs=[hbm()] + [vmem()] * 2 + [hbm()],
        scratch_shapes=index_scratch
        + [
            pltpu.SMEM((line,), F32),
            acc,
            pltpu.VMEM((stencil * room, LANES), F32),
            column_slots,
        ]
        + work,
        compiler_params=params(),
        name="apply_first",
    )(meta, ints, floats, own_lines, own, std, std_l, std_r, lat2, lon2)

    replies = lax.all_to_all(message, "pencil", split_axis=0, concat_axis=0, tiled=True)
    back = replies.reshape(-1)
    line_rows = LISTED // LANES * (stencil + 8)
    row_lines, row_data = pl.pallas_call(
        functools.partial(list_kernel, **place),
        out_shape=[
            jax.ShapeDtypeStruct((line_rows, LANES), I32),
            jax.ShapeDtypeStruct((LISTED, LANES), F32),
        ],
        in_specs=[smem(), vmem(), hbm()],
        out_specs=[vmem()] * 2,
        scratch_shapes=[pltpu.VMEM((STACK, LISTED), F32)],
        compiler_params=params(),
        cost_estimate=cost(4000),
        name="list_rows",
    )(meta, recv, info)
    row_lines = row_lines.reshape(-1)

    field1, sums = pl.pallas_call(
        functools.partial(apply_kernel, first=False, **static),
        out_shape=[
            field_shape,
            jax.ShapeDtypeStruct((parts * levels, 8, LANES), F32),
        ],
        in_specs=[smem()] + [hbm()] * 3 + [vmem(), hbm(), vmem()] + [hbm()] * 7,
        out_specs=[hbm(), vmem()],
        scratch_shapes=index_scratch + [pltpu.SMEM((parts * slots,), F32)] + work,
        compiler_params=params(),
        name="apply_second",
    )(
        meta,
        ints,
        floats,
        own_lines,
        info,
        back,
        replies,
        std,
        std_l,
        std_r,
        lat2,
        lon2,
        merged,
        row_data,
    )

    totals = lax.all_to_all(sums, ("pencil", "lev"), split_axis=0, concat_axis=0, tiled=True)
    totals = totals.reshape(parts, levels, 8, LANES)

    listed_rows, mixed = pl.pallas_call(
        functools.partial(factor_kernel, stencil=stencil, slots=slots),
        out_shape=[
            jax.ShapeDtypeStruct((stencil * LISTED, LANES), F32),
            jax.ShapeDtypeStruct((LISTED, LANES), F32),
        ],
        in_specs=[hbm(), vmem(), vmem(), hbm()],
        out_specs=[hbm(), vmem()],
        scratch_shapes=[
            pltpu.SMEM((line_rows * LANES,), I32),
            pltpu.VMEM((parts * slots, LANES), F32),
            pltpu.VMEM((stencil * LISTED, LANES), F32),
            pltpu.SemaphoreType.DMA((3,)),
        ],
        compiler_params=params(),
        cost_estimate=cost(8000),
        name="factor_rows",
    )(row_lines, row_data, replies, sums)

    by_chunk = back
    if chunks > 1:
        by_chunk = jnp.concatenate(
            [replies[:, : slots // LANES, :], replies[:, 8:, :]], axis=1
        ).reshape(parts, stencil + 1, chunks, group * capacity)
        by_chunk = jnp.transpose(by_chunk, (2, 0, 1, 3)).reshape(-1)
    owner_words = by_chunk.shape[0] // (chunks * parts)
    high_rows = rows_block + 2 * PAD
    acc_rows = pltpu.VMEM(((length // LANES) * high_rows + 8, LANES), F32)
    control, increment = pl.pallas_call(
        functools.partial(
            final_kernel,
            layout=layout,
            hold=hold,
            stencil=stencil,
            capacity=capacity,
            senders=senders,
            parts=parts,
            length=length,
        ),
        out_shape=[
            jax.ShapeDtypeStruct((rows_block, length), F32),
            field_shape,
        ],
        in_specs=[hbm()] * 5 + [vmem()] * 2 + [hbm()] * 2 + [vmem()] * 2,
        out_specs=[hbm()] * 2,
        scratch_shapes=[
            pltpu.SMEM((per,), I32),
            pltpu.SMEM((line,), I32),
            pltpu.SMEM((line,), I32),
            pltpu.SMEM((line,), F32),
            pltpu.SMEM((parts * owner_words,), F32),
            pltpu.VMEM((columns, height), F32),
            pltpu.VMEM((columns, height), F32),
            pltpu.VMEM((rows_block, length), F32),
            pltpu.VMEM((rows_block, length), BF),
            pltpu.VMEM((rows_block, length), BF),
            pltpu.SMEM((line_rows * LANES,), I32),
            pltpu.VMEM((stencil * LISTED, LANES), F32),
            pltpu.VMEM((LISTED, LANES), F32),
        ]
        + [acc_rows] * PAIR
        + [
            pltpu.SemaphoreType.DMA((5,)),
            pltpu.SemaphoreType.DMA((5,)),
            pltpu.SemaphoreType.DMA((1 + length // WIDE,)),
        ],
        compiler_params=params(),
        name="outputs",
    )(
        ints,
        floats,
        by_chunk,
        row_lines,
        listed_rows,
        mixed,
        totals,
        field0,
        field1,
        lat1,
        lon1,
    )
    return control[None], increment[None]


def solution(mesh):
    return jax.shard_map(
        body,
        mesh=mesh,
        in_specs=(
            P("lev", "pencil", None),
            P("lev", None),
            P("lev", None),
            P(("pencil", "lev"), None),
            P(("pencil", "lev"), None),
            P(("pencil", "lev"), None),
            P(("pencil", "lev")),
            P(("pencil", "lev")),
            P(("pencil", "lev")),
        ),
        out_specs=(P("lev", "pencil", None), P("lev", "pencil", None)),
        check_vma=False,
    )
```

profile of v0, /device:TPU:0, one launch (start us, length us, event | category | flops | bytes accessed | tf_op | source)
XLA Modules:
  0.0 117.5 jit_solution(16733204892952720386)
XLA Ops:
  1.3 2.2 %pack.1 = f32[8,40,256]{2,1,0:T(8,128)} custom-call(s32[1]{0:T(128)S(6)} %copy.11.counts, s32[1,256]{1,0:T(1,128)} %bitcast.38, s32[16,256]{1,0:T(8,128)} %bitcast.36, f32[16,256]{1,0:T(8,128)} %bitcast.37, f32[1,256]{1,0:T(1,128)} %bitcast.39, f32[1,256]{1,0:T(1,128)} %bitcast.40), custom_call_target="tpu_custom_call" | custom-call | bytes 44280000 | tf_op jit(solution)/shard_map/pack/pallas_call | solution.py:1292
  3.4 7.3 %all-to-all-start = ((f32[8,40,256]{2,1,0:T(8,128)}), f32[8,40,256]{2,1,0:T(8,128)S(1)}, u32[]{:S(2)}, u32[]{:S(2)}) async-start(f32[8,40,256]{2,1,0:T(8,128)} %pack.1), calls=%async_computation | async-start | bytes 655360 | tf_op jit(solution)/shard_map/all_to_all | solution.py:1311
  10.7 1.1 slice_bitcast_fusion
  11.8 4.8 %collective-permute-start.1 = (f32[32,2048]{1,0:T(8,128)S(1)}, f32[32,2048]{1,0:T(8,128)S(1)}, u32[]{:S(2)}, u32[]{:S(2)}) collective-permute-start(f32[32,2048]{1,0:T(8,128)S(1)} %get-tuple-element.42), channel_id=1, source_target_pairs={{0,28},{4,0},{8,4},{12,8},{16,12},{20,16},{24,20},{28,24},{1,29},{... | collective-permute-start | bytes 786440 | tf_op jit(solution)/shard_map/ppermute | solution.py:1316
  16.6 0.0 collective-permute-start
  16.6 6.3 %bands.1 = (bf16[2,3,512,256]{3,2,1,0:T(8,128)(2,1)}, bf16[2,192,256]{2,1,0:T(8,128)(2,1)}, bf16[2,128,160]{2,1,0:T(8,128)(2,1)}, bf16[2,512,256]{2,1,0:T(8,128)(2,1)}) custom-call(f32[31]{0:T(128)} %bitcast.43, f32[31]{0:T(128)} %bitcast.44), custom_call_target="tpu_custom_call" | custom-call | bytes 369000 | tf_op jit(solution)/shard_map/bands/pallas_call | solution.py:1320
  22.8 0.0 all-to-all-done.recv
  22.8 0.0 copy-start.1
  22.8 0.7 copy-done.1
  23.6 3.5 %unpack.1 = (s32[592,128]{1,0:T(8,128)}, f32[272,128]{1,0:T(8,128)}, s32[120,128]{1,0:T(8,128)}, f32[640,128]{1,0:T(8,128)}) custom-call(s32[1]{0:T(128)} %bitcast.meta.refs_0_, f32[8,40,256]{2,1,0:T(8,128)} %copy-done.1, bf16[2,128,160]{2,1,0:T(8,128)(2,1)} %get-tuple-element.22._.lat1), custom_call_target="tpu_custom_call" | custom-call | bytes 369000 | tf_op jit(solution)/shard_map/unpack/pallas_call | solution.py:1339
  27.1 1.2 %collective-permute-done.1.refs_7_.refs_9_ = f32[32,2048]{1,0:T(8,128)S(1)} collective-permute-done((f32[32,2048]{1,0:T(8,128)S(1)}, f32[32,2048]{1,0:T(8,128)S(1)}, u32[]{:S(2)}, u32[]{:S(2)}) %collective-permute-start.1) | collective-permute-done | bytes 262176 | tf_op jit(solution)/shard_map/ppermute | solution.py:1316
  28.3 0.0 copy-start.2
  28.3 0.0 collective-permute-done.refs_6_.refs_8_
  28.3 0.0 copy-start.3
  28.3 0.7 copy-done.2
  29.0 0.1 copy-done.3
  29.1 19.7 %apply_first.1 = (f32[512,2048]{1,0:T(8,128)}, f32[8,72,128]{2,1,0:T(8,128)}, f32[640,128]{1,0:T(8,128)}, f32[10240,128]{1,0:T(8,128)}) custom-call(s32[1]{0:T(128)} %bitcast.meta.refs_0_, s32[75776]{0:T(1024)} %bitcast.25, f32[34816]{0:T(1024)} %bitcast.28, s32[15360]{0:T(1024)} %bitcast.32, f32[640,128]{1,0:T(8,128)} %get-tuple-element.26.refs_4_, ...), custom_call_target="tpu_custom_call" | custom-call | tf_op jit(solution)/shard_map/apply_first/pallas_call | solution.py:1406
  48.8 16.0 %all-to-all-start.1 = ((f32[8,72,128]{2,1,0:T(8,128)}), f32[8,72,128]{2,1,0:T(8,128)S(1)}, u32[]{:S(2)}, u32[]{:S(2)}) async-start(f32[8,72,128]{2,1,0:T(8,128)} %get-tuple-element.29), calls=%async_computation.1 | async-start | bytes 589824 | tf_op jit(solution)/shard_map/all_to_all | solution.py:1428
  64.8 4.0 %list_rows.1 = (s32[96,128]{1,0:T(8,128)}, f32[512,128]{1,0:T(8,128)}) custom-call(s32[1]{0:T(128)} %bitcast.meta.refs_0_, f32[8,40,256]{2,1,0:T(8,128)} %copy-done.1, f32[640,128]{1,0:T(8,128)} %get-tuple-element.30._.refs_4_), custom_call_target="tpu_custom_call" | custom-call | bytes 14760000 | tf_op jit(solution)/shard_map/list_rows/pallas_call | solution.py:1431
  68.7 4.5 %all-to-all-done.1.refs_6_.replies = f32[8,72,128]{2,1,0:T(8,128)S(1)} async-done(((f32[8,72,128]{2,1,0:T(8,128)}), f32[8,72,128]{2,1,0:T(8,128)S(1)}, u32[]{:S(2)}, u32[]{:S(2)}) %all-to-all-start.1) | async-done | bytes 294944 | tf_op jit(solution)/shard_map/all_to_all | solution.py:1428
  73.2 0.0 copy-start
  73.2 0.7 copy-done
  73.9 14.1 %apply_second.1 = (f32[512,2048]{1,0:T(8,128)}, f32[32,8,128]{2,1,0:T(8,128)}) custom-call(s32[1]{0:T(128)} %bitcast.meta.refs_0_, s32[75776]{0:T(1024)} %bitcast.26, f32[34816]{0:T(1024)} %bitcast.29, s32[15360]{0:T(1024)} %bitcast.33, f32[640,128]{1,0:T(8,128)} %get-tuple-element.30._.refs_4_, f32[73728]{0:T(1024)} %bitcast.23, f32[8,72,128]{2,1,0:T(8,128)} %copy-done, ...), custom_call_target="tpu_custom_call" | custom-call | tf_op jit(solution)/shard_map/apply_second/pallas_call | solution.py:1446
  88.0 8.1 %all-to-all-start.2 = ((f32[32,8,128]{2,1,0:T(8,128)}), f32[32,8,128]{2,1,0:T(8,128)S(1)}, u32[]{:S(2)}, u32[]{:S(2)}) async-start(f32[32,8,128]{2,1,0:T(8,128)} %get-tuple-element.34._), calls=%async_computation.2 | async-start | bytes 262144 | tf_op jit(solution)/shard_map/all_to_all | solution.py:1474
  96.1 7.8 %factor_rows.1 = (f32[8192,128]{1,0:T(8,128)}, f32[512,128]{1,0:T(8,128)}) custom-call(s32[12288]{0:T(1024)} %bitcast.34, f32[512,128]{1,0:T(8,128)} %get-tuple-element.32.refs_13_.data, f32[8,72,128]{2,1,0:T(8,128)} %copy-done, f32[32,8,128]{2,1,0:T(8,128)} %get-tuple-element.34._), custom_call_target="tpu_custom_call" | custom-call | bytes 29520000 | tf_op jit(solution)/shard_map/factor_rows/pallas_call | solution.py:1477
  103.9 0.4 all-to-all-done.2
  104.3 0.0 copy-start.4
  104.3 0.6 copy-done.4
  105.0 12.3 %outputs.1 = (f32[256,4096]{1,0:T(8,128)}, f32[512,2048]{1,0:T(8,128)}) custom-call(s32[75776]{0:T(1024)} %bitcast.27, f32[34816]{0:T(1024)} %bitcast.30, f32[73728]{0:T(1024)} %bitcast.24, s32[12288]{0:T(1024)} %bitcast.35, f32[8192,128]{1,0:T(8,128)} %get-tuple-element.35.merged_h, f32[512,128]{1,0:T(8,128)} %get-tuple-element.36.mixed, ...), custom_call_target="tpu_custom_call" | custom-call | tf_op jit(solution)/shard_map/outputs/pallas_call | solution.py:1505
Async XLA Ops:
  3.4 19.4 %all-to-all-start = ((f32[8,40,256]{2,1,0:T(8,128)}), f32[8,40,256]{2,1,0:T(8,128)S(1)}, u32[]{:S(2)}, u32[]{:S(2)}) async-start(f32[8,40,256]{2,1,0:T(8,128)} %pack.1), calls=%async_computation | async-start | bytes 655360 | tf_op jit(solution)/shard_map/all_to_all | solution.py:1311
  11.8 16.5 %collective-permute-start.1 = (f32[32,2048]{1,0:T(8,128)S(1)}, f32[32,2048]{1,0:T(8,128)S(1)}, u32[]{:S(2)}, u32[]{:S(2)}) collective-permute-start(f32[32,2048]{1,0:T(8,128)S(1)} %get-tuple-element.42), channel_id=1, source_target_pairs={{0,28},{4,0},{8,4},{12,8},{16,12},{20,16},{24,20},{28,24},{1,29},{... | collective-permute-start | bytes 786440 | tf_op jit(solution)/shard_map/ppermute | solution.py:1316
  16.6 11.7 %collective-permute-start = (f32[32,2048]{1,0:T(8,128)S(1)}, f32[32,2048]{1,0:T(8,128)S(1)}, u32[]{:S(2)}, u32[]{:S(2)}) collective-permute-start(f32[32,2048]{1,0:T(8,128)S(1)} %get-tuple-element.43), channel_id=1, source_target_pairs={{0,4},{4,8},{8,12},{12,16},{16,20},{20,24},{24,28},{28,0},{1,5},{5... | collective-permute-start | bytes 786440 | tf_op jit(solution)/shard_map/ppermute | solution.py:1315
  22.8 0.7 copy-start.1
  28.3 0.7 copy-start.2
  28.3 0.8 copy-start.3
  48.8 24.4 %all-to-all-start.1 = ((f32[8,72,128]{2,1,0:T(8,128)}), f32[8,72,128]{2,1,0:T(8,128)S(1)}, u32[]{:S(2)}, u32[]{:S(2)}) async-start(f32[8,72,128]{2,1,0:T(8,128)} %get-tuple-element.29), calls=%async_computation.1 | async-start | bytes 589824 | tf_op jit(solution)/shard_map/all_to_all | solution.py:1428
  73.2 0.7 copy-start
  88.0 16.3 %all-to-all-start.2 = ((f32[32,8,128]{2,1,0:T(8,128)}), f32[32,8,128]{2,1,0:T(8,128)S(1)}, u32[]{:S(2)}, u32[]{:S(2)}) async-start(f32[32,8,128]{2,1,0:T(8,128)} %get-tuple-element.34._), calls=%async_computation.2 | async-start | bytes 262144 | tf_op jit(solution)/shard_map/all_to_all | solution.py:1474
  104.3 0.6 copy-start.4
where the time goes:
time: 119 us; the launch traced here: 117 us
  Pallas kernels  69.7 us (59%)
  starting transfers between devices  36.1 us (30%)
  waiting for transfers between devices  6.17 us (5%)
  local copies, waits for them, and re-layouts  3.96 us (3%)
  between operations  1.53 us (1%)
    pallas_call x1, Pallas kernels, body(): pl.pallas_call(functools.partial(apply_kernel, first=True, **static), out...  19.7 us
    all_to_all x1, starting transfers between devices, body(): lax.all_to_all(message, 'pencil', split_axis=0, concat_axis=0, tiled=True)  16 us
    pallas_call x1, Pallas kernels, body(): pl.pallas_call(functools.partial(apply_kernel, first=False, **static), ou...  14.1 us
    pallas_call x1, Pallas kernels, body(): pl.pallas_call(functools.partial(final_kernel, layout=layout, hold=hold,...  12.3 us
    all_to_all x1, starting transfers between devices, body(): lax.all_to_all(sums, ('pencil', 'lev'), split_axis=0, concat_axis=0, tile...  8.07 us
    pallas_call x1, Pallas kernels, body(): pl.pallas_call(functools.partial(factor_kernel, stencil=stencil, slots=sl...  7.77 us
    all_to_all x1, starting transfers between devices, body(): lax.all_to_all(packed, 'pencil', split_axis=0, concat_axis=0, tiled=True)  7.28 us
    pallas_call x1, Pallas kernels, body(): pl.pallas_call(functools.partial(bands_kernel, rows_block=row_size), out_...  6.26 us
  transfers between devices with their start and end apart: 5, of which 3 were waited for; matrix products, arithmetic and copies ran while one was open for 1% of the time, Pallas kernels for 18%

commit v1 on v0

--- a/solution.py
+++ b/solution.py
@@ -1201,9 +1201,7 @@
     for copy in operands:
         copy.wait()
     increment = field0
-    increment[...] = first * field0[...] + second * field1[...]
-    outgoing = [pltpu.make_async_copy(increment, increment_h, out_sems.at[0])]
-    outgoing[0].start()
+    outgoing = []
 
     pair = WIDE // LANES
     count = length // WIDE
@@ -1235,18 +1233,26 @@
 
     every_lanes = 4
 
+    def send_out(source, target, block, size):
+        if block % every_lanes == every_lanes - 1:
+            lanes = slice((block + 1 - every_lanes) * size, (block + 1) * size)
+            copy = pltpu.make_async_copy(
+                source.at[:, lanes], target.at[:, lanes], out_sems.at[len(outgoing)]
+            )
+            copy.start()
+            outgoing.append(copy)
+
+    def combine(block):
+        size = increment.shape[1] // count
+        lanes = slice(block * size, (block + 1) * size)
+        increment[:, lanes] = first * field0[:, lanes] + second * field1[:, lanes]
+        send_out(increment, increment_h, block, size)
+
     def along_longitude(block):
         control[:, block * WIDE : (block + 1) * WIDE] = mm_parts(
             (window(high_s, block), window(low_s, block)), (lon1[0], lon1[1])
         )
-        if block % every_lanes == every_lanes - 1:
-            lanes = slice((block + 1 - every_lanes) * WIDE, (block + 1) * WIDE)
-            outgoing.append(
-                pltpu.make_async_copy(
-                    control.at[:, lanes], control_h.at[:, lanes], out_sems.at[len(outgoing)]
-                )
-            )
-            outgoing[-1].start()
+        send_out(control, control_h, block, WIDE)
 
     along_latitude(count - 1)
     along_latitude(0)
@@ -1254,6 +1260,7 @@
     for block in range(count):
         if 2 <= block + 2 < count - 1:
             along_latitude(block + 2)
+        combine(block)
         along_longitude(block)
     for copy in outgoing:
         copy.wait()

time: 119 us -> 122 us (1.025)
  Pallas kernels: 69.7 us -> 72.4 us
    all_to_all x1, starting transfers between devices: 16 us -> 17.3 us  [body(): lax.all_to_all(message, 'pencil', split_axis=0, concat_axis=0, tiled=True)]
  transfers between devices with their start and end apart: 5 -> 5, of which waited for: 3 -> 2; matrix products, arithmetic and copies ran while one was open for 1% -> 1% of each run, Pallas kernels for 18% -> 18%
where the time goes in v1:
time: 122 us; the launch traced here: 121 us
  Pallas kernels  72.4 us (59%)
  starting transfers between devices  37.1 us (30%)
  waiting for transfers between devices  6.05 us (5%)
  local copies, waits for them, and re-layouts  3.95 us (3%)
  between operations  1.55 us (1%)
    pallas_call x1, Pallas kernels, body(): pl.pallas_call(functools.partial(apply_kernel, first=True, **static), out...  20.1 us
    all_to_all x1, starting transfers between devices, body(): lax.all_to_all(message, 'pencil', split_axis=0, concat_axis=0, tiled=True)  17.3 us
    pallas_call x1, Pallas kernels, body(): pl.pallas_call(functools.partial(apply_kernel, first=False, **static), ou...  14.7 us
    pallas_call x1, Pallas kernels, body(): pl.pallas_call(functools.partial(final_kernel, layout=layout, hold=hold,...  13.4 us
    pallas_call x1, Pallas kernels, body(): pl.pallas_call(functools.partial(factor_kernel, stencil=stencil, slots=sl...  8.39 us
    all_to_all x1, starting transfers between devices, body(): lax.all_to_all(sums, ('pencil', 'lev'), split_axis=0, concat_axis=0, tile...  7.79 us
    all_to_all x1, starting transfers between devices, body(): lax.all_to_all(packed, 'pencil', split_axis=0, concat_axis=0, tiled=True)  7.28 us
    pallas_call x1, Pallas kernels, body(): pl.pallas_call(functools.partial(bands_kernel, rows_block=row_size), out_...  6.26 us
  transfers between devices with their start and end apart: 5, of which 2 were waited for; matrix products, arithmetic and copies ran while one was open for 1% of the time, Pallas kernels for 18%

profile of v1, /device:TPU:0, one launch (start us, length us, event | category | flops | bytes accessed | tf_op | source)
XLA Modules:
  0.0 121.1 jit_solution(16699257757275177496)
XLA Ops:
  1.3 2.2 %pack.1 = f32[8,40,256]{2,1,0:T(8,128)} custom-call(s32[1]{0:T(128)S(6)} %copy.11.counts, s32[1,256]{1,0:T(1,128)} %bitcast.38, s32[16,256]{1,0:T(8,128)} %bitcast.36, f32[16,256]{1,0:T(8,128)} %bitcast.37, f32[1,256]{1,0:T(1,128)} %bitcast.39, f32[1,256]{1,0:T(1,128)} %bitcast.40), custom_call_target="tpu_custom_call" | custom-call | bytes 44280000 | tf_op jit(solution)/shard_map/pack/pallas_call | solution.py:1299
  3.4 7.3 %all-to-all-start = ((f32[8,40,256]{2,1,0:T(8,128)}), f32[8,40,256]{2,1,0:T(8,128)S(1)}, u32[]{:S(2)}, u32[]{:S(2)}) async-start(f32[8,40,256]{2,1,0:T(8,128)} %pack.1), calls=%async_computation | async-start | bytes 655360 | tf_op jit(solution)/shard_map/all_to_all | solution.py:1318
  10.7 1.1 slice_bitcast_fusion
  11.8 4.8 %collective-permute-start.1 = (f32[32,2048]{1,0:T(8,128)S(1)}, f32[32,2048]{1,0:T(8,128)S(1)}, u32[]{:S(2)}, u32[]{:S(2)}) collective-permute-start(f32[32,2048]{1,0:T(8,128)S(1)} %get-tuple-element.42), channel_id=1, source_target_pairs={{0,28},{4,0},{8,4},{12,8},{16,12},{20,16},{24,20},{28,24},{1,29},{... | collective-permute-start | bytes 786440 | tf_op jit(solution)/shard_map/ppermute | solution.py:1323
  16.6 0.0 collective-permute-start
  16.6 6.3 %bands.1 = (bf16[2,3,512,256]{3,2,1,0:T(8,128)(2,1)}, bf16[2,192,256]{2,1,0:T(8,128)(2,1)}, bf16[2,128,160]{2,1,0:T(8,128)(2,1)}, bf16[2,512,256]{2,1,0:T(8,128)(2,1)}) custom-call(f32[31]{0:T(128)} %bitcast.43, f32[31]{0:T(128)} %bitcast.44), custom_call_target="tpu_custom_call" | custom-call | bytes 369000 | tf_op jit(solution)/shard_map/bands/pallas_call | solution.py:1327
  22.8 0.0 all-to-all-done.recv
  22.8 0.0 copy-start.1
  22.8 0.7 copy-done.1
  23.6 3.5 %unpack.1 = (s32[592,128]{1,0:T(8,128)}, f32[272,128]{1,0:T(8,128)}, s32[120,128]{1,0:T(8,128)}, f32[640,128]{1,0:T(8,128)}) custom-call(s32[1]{0:T(128)} %bitcast.meta.refs_0_, f32[8,40,256]{2,1,0:T(8,128)} %copy-done.1, bf16[2,128,160]{2,1,0:T(8,128)(2,1)} %get-tuple-element.22._.lat1), custom_call_target="tpu_custom_call" | custom-call | bytes 369000 | tf_op jit(solution)/shard_map/unpack/pallas_call | solution.py:1346
  27.1 1.2 %collective-permute-done.1.refs_7_.refs_9_ = f32[32,2048]{1,0:T(8,128)S(1)} collective-permute-done((f32[32,2048]{1,0:T(8,128)S(1)}, f32[32,2048]{1,0:T(8,128)S(1)}, u32[]{:S(2)}, u32[]{:S(2)}) %collective-permute-start.1) | collective-permute-done | bytes 262176 | tf_op jit(solution)/shard_map/ppermute | solution.py:1323
  28.3 0.0 copy-start.2
  28.3 0.0 collective-permute-done.refs_6_.refs_8_
  28.3 0.0 copy-start.3
  28.3 0.7 copy-done.2
  29.0 0.1 copy-done.3
  29.1 20.1 %apply_first.1 = (f32[512,2048]{1,0:T(8,128)}, f32[8,72,128]{2,1,0:T(8,128)}, f32[640,128]{1,0:T(8,128)}, f32[10240,128]{1,0:T(8,128)}) custom-call(s32[1]{0:T(128)} %bitcast.meta.refs_0_, s32[75776]{0:T(1024)} %bitcast.25, f32[34816]{0:T(1024)} %bitcast.28, s32[15360]{0:T(1024)} %bitcast.32, f32[640,128]{1,0:T(8,128)} %get-tuple-element.26.refs_4_, ...), custom_call_target="tpu_custom_call" | custom-call | tf_op jit(solution)/shard_map/apply_first/pallas_call | solution.py:1413
  49.2 17.3 %all-to-all-start.1 = ((f32[8,72,128]{2,1,0:T(8,128)}), f32[8,72,128]{2,1,0:T(8,128)S(1)}, u32[]{:S(2)}, u32[]{:S(2)}) async-start(f32[8,72,128]{2,1,0:T(8,128)} %get-tuple-element.29), calls=%async_computation.1 | async-start | bytes 589824 | tf_op jit(solution)/shard_map/all_to_all | solution.py:1435
  66.5 4.0 %list_rows.1 = (s32[96,128]{1,0:T(8,128)}, f32[512,128]{1,0:T(8,128)}) custom-call(s32[1]{0:T(128)} %bitcast.meta.refs_0_, f32[8,40,256]{2,1,0:T(8,128)} %copy-done.1, f32[640,128]{1,0:T(8,128)} %get-tuple-element.30._.refs_4_), custom_call_target="tpu_custom_call" | custom-call | bytes 14760000 | tf_op jit(solution)/shard_map/list_rows/pallas_call | solution.py:1438
  70.4 4.8 %all-to-all-done.1.refs_6_.replies = f32[8,72,128]{2,1,0:T(8,128)S(1)} async-done(((f32[8,72,128]{2,1,0:T(8,128)}), f32[8,72,128]{2,1,0:T(8,128)S(1)}, u32[]{:S(2)}, u32[]{:S(2)}) %all-to-all-start.1) | async-done | bytes 294944 | tf_op jit(solution)/shard_map/all_to_all | solution.py:1435
  75.2 0.0 copy-start
  75.2 0.7 copy-done
  75.9 14.7 %apply_second.1 = (f32[512,2048]{1,0:T(8,128)}, f32[32,8,128]{2,1,0:T(8,128)}) custom-call(s32[1]{0:T(128)} %bitcast.meta.refs_0_, s32[75776]{0:T(1024)} %bitcast.26, f32[34816]{0:T(1024)} %bitcast.29, s32[15360]{0:T(1024)} %bitcast.33, f32[640,128]{1,0:T(8,128)} %get-tuple-element.30._.refs_4_, f32[73728]{0:T(1024)} %bitcast.23, f32[8,72,128]{2,1,0:T(8,128)} %copy-done, ...), custom_call_target="tpu_custom_call" | custom-call | tf_op jit(solution)/shard_map/apply_second/pallas_call | solution.py:1453
  90.7 7.8 %all-to-all-start.2 = ((f32[32,8,128]{2,1,0:T(8,128)}), f32[32,8,128]{2,1,0:T(8,128)S(1)}, u32[]{:S(2)}, u32[]{:S(2)}) async-start(f32[32,8,128]{2,1,0:T(8,128)} %get-tuple-element.34._), calls=%async_computation.2 | async-start | bytes 262144 | tf_op jit(solution)/shard_map/all_to_all | solution.py:1481
  98.5 8.4 %factor_rows.1 = (f32[8192,128]{1,0:T(8,128)}, f32[512,128]{1,0:T(8,128)}) custom-call(s32[12288]{0:T(1024)} %bitcast.34, f32[512,128]{1,0:T(8,128)} %get-tuple-element.32.refs_13_.data, f32[8,72,128]{2,1,0:T(8,128)} %copy-done, f32[32,8,128]{2,1,0:T(8,128)} %get-tuple-element.34._), custom_call_target="tpu_custom_call" | custom-call | bytes 29520000 | tf_op jit(solution)/shard_map/factor_rows/pallas_call | solution.py:1484
  106.9 0.0 all-to-all-done.2
  106.9 0.0 copy-start.4
  106.9 0.6 copy-done.4
  107.5 13.4 %outputs.1 = (f32[256,4096]{1,0:T(8,128)}, f32[512,2048]{1,0:T(8,128)}) custom-call(s32[75776]{0:T(1024)} %bitcast.27, f32[34816]{0:T(1024)} %bitcast.30, f32[73728]{0:T(1024)} %bitcast.24, s32[12288]{0:T(1024)} %bitcast.35, f32[8192,128]{1,0:T(8,128)} %get-tuple-element.35.merged_h, f32[512,128]{1,0:T(8,128)} %get-tuple-element.36.mixed, ...), custom_call_target="tpu_custom_call" | custom-call | tf_op jit(solution)/shard_map/outputs/pallas_call | solution.py:1512
Async XLA Ops:
  3.4 19.4 %all-to-all-start = ((f32[8,40,256]{2,1,0:T(8,128)}), f32[8,40,256]{2,1,0:T(8,128)S(1)}, u32[]{:S(2)}, u32[]{:S(2)}) async-start(f32[8,40,256]{2,1,0:T(8,128)} %pack.1), calls=%async_computation | async-start | bytes 655360 | tf_op jit(solution)/shard_map/all_to_all | solution.py:1318
  11.8 16.5 %collective-permute-start.1 = (f32[32,2048]{1,0:T(8,128)S(1)}, f32[32,2048]{1,0:T(8,128)S(1)}, u32[]{:S(2)}, u32[]{:S(2)}) collective-permute-start(f32[32,2048]{1,0:T(8,128)S(1)} %get-tuple-element.42), channel_id=1, source_target_pairs={{0,28},{4,0},{8,4},{12,8},{16,12},{20,16},{24,20},{28,24},{1,29},{... | collective-permute-start | bytes 786440 | tf_op jit(solution)/shard_map/ppermute | solution.py:1323
  16.6 11.7 %collective-permute-start = (f32[32,2048]{1,0:T(8,128)S(1)}, f32[32,2048]{1,0:T(8,128)S(1)}, u32[]{:S(2)}, u32[]{:S(2)}) collective-permute-start(f32[32,2048]{1,0:T(8,128)S(1)} %get-tuple-element.43), channel_id=1, source_target_pairs={{0,4},{4,8},{8,12},{12,16},{16,20},{20,24},{24,28},{28,0},{1,5},{5... | collective-permute-start | bytes 786440 | tf_op jit(solution)/shard_map/ppermute | solution.py:1322
  22.8 0.7 copy-start.1
  28.3 0.7 copy-start.2
  28.3 0.8 copy-start.3
  49.2 26.0 %all-to-all-start.1 = ((f32[8,72,128]{2,1,0:T(8,128)}), f32[8,72,128]{2,1,0:T(8,128)S(1)}, u32[]{:S(2)}, u32[]{:S(2)}) async-start(f32[8,72,128]{2,1,0:T(8,128)} %get-tuple-element.29), calls=%async_computation.1 | async-start | bytes 589824 | tf_op jit(solution)/shard_map/all_to_all | solution.py:1435
  75.2 0.7 copy-start
  90.7 16.2 %all-to-all-start.2 = ((f32[32,8,128]{2,1,0:T(8,128)}), f32[32,8,128]{2,1,0:T(8,128)S(1)}, u32[]{:S(2)}, u32[]{:S(2)}) async-start(f32[32,8,128]{2,1,0:T(8,128)} %get-tuple-element.34._), calls=%async_computation.2 | async-start | bytes 262144 | tf_op jit(solution)/shard_map/all_to_all | solution.py:1481
  106.9 0.6 copy-start.4
